TPU v7x, 32 devices: a whole 2x2x4 slice. The times are simulated.
32 devices in a mesh: gx: 2 (over y), gy: 4 (over x, core), gz: 4 (over z).
Axes of the slice: x: 2, y: 2, z: 4, core: 2. Of those that a mesh axis runs over, the one named last changes fastest.
Arguments:
- iterate: float32 [16, 64, 512], P('gx', 'gy', 'gz'), may hold values from -6 to 6
- source: float32 [16, 64, 512], P('gx', 'gy', 'gz'), may hold values from -6 to 6
- permeability: float32 [16, 64, 512], P('gx', 'gy', 'gz'), may hold values from 0.1 to 10
- storage: float32 [16, 64, 512], P('gx', 'gy', 'gz'), may hold values from 0.01 to 0.1
Outputs:
- updated: float32 [16, 64, 512], P('gx', 'gy', 'gz')
All inputs are finite; a program needn't handle non-finite values.
Results may differ from a plain program's by a relative error of at most 0.0003.
Values sent between devices are 32-bit elements; how exact they have to be, the bound alone decides.
A program may use at most 64 MiB of HBM per device.

v0:
```python
import jax
import jax.numpy as jnp
from jax import lax
from jax.sharding import PartitionSpec as P

MARGIN = 3
COARSEN = 8
NEWTON = 2
SWEEPS = 4
CSWEEPS = 6


def with_halo(x, sides, width):
    for axis, dim in sides:
        devices, length = (lax.axis_size(axis), x.shape[dim])
        up = [(i, (i + 1) % devices) for i in range(devices)]
        down = [(j, i) for i, j in up]
        last = lax.slice_in_dim(x, length - width, length, axis=dim)
        initial = lax.slice_in_dim(x, 0, width, axis=dim)
        before = lax.ppermute(last, axis, up)
        after = lax.ppermute(initial, axis, down)
        x = jnp.concatenate([before, x, after], axis=dim)
    return x


def cut(array, axis, piece, rest):
    index = [rest, rest, rest]
    index[axis] = piece
    return array[tuple(index)]


def face_partitions(padded, coef_pad, inv):
    partition_list = []
    diffs = []
    for axis in range(3):
        upper = cut(padded, axis, slice(1, None), slice(1, -1))
        lower = cut(padded, axis, slice(0, -1), slice(1, -1))
        kupper = cut(coef_pad, axis, slice(1, None), slice(1, -1))
        klower = cut(coef_pad, axis, slice(0, -1), slice(1, -1))
        diff = upper - lower
        scaled = diff * inv
        coef = 0.5 * (kupper + klower) * (1.0 + scaled * scaled) ** (-0.25) * (inv * inv)
        partition_list.append(coef)
        diffs.append(diff)
    flow_operator = 0.0
    partition_weight = 0.0
    for axis in range(3):
        flux = partition_list[axis] * diffs[axis]
        flow_operator = (
            flow_operator
            + cut(flux, axis, slice(1, None), slice(None))
            - cut(flux, axis, slice(0, -1), slice(None))
        )
        partition_weight = (
            partition_weight
            + cut(partition_list[axis], axis, slice(1, None), slice(None))
            + cut(partition_list[axis], axis, slice(0, -1), slice(None))
        )
    return (partition_list, flow_operator, partition_weight)


def neighbour(partition_list, delta_pad):
    total = 0.0
    for axis in range(3):
        total = total + cut(partition_list[axis], axis, slice(1, None), slice(None)) * cut(
            delta_pad, axis, slice(2, None), slice(1, -1)
        )
        total = total + cut(partition_list[axis], axis, slice(0, -1), slice(None)) * cut(
            delta_pad, axis, slice(0, -2), slice(1, -1)
        )
    return total


def local_subdomain_newton(value_padded, permeability_padded, reaction_term, right_hand_side):
    interior_region = value_padded[1:-1, 1:-1, 1:-1]
    for step in range(NEWTON):
        partition_list, flow_operator, partition_weight = face_partitions(
            value_padded, permeability_padded, 1.0
        )
        res = right_hand_side - reaction_term * interior_region + flow_operator
        diag = reaction_term + partition_weight
        delta = res / diag
        for sweep in range(SWEEPS - 1):
            delta = (res + neighbour(partition_list, jnp.pad(delta, 1))) / diag
        interior_region = interior_region + delta
        value_padded = value_padded.at[1:-1, 1:-1, 1:-1].set(interior_region)
    return interior_region


def restrict(field):
    a, b, c = field.shape
    grouped = field.reshape(a // COARSEN, COARSEN, b // COARSEN, COARSEN, c // COARSEN, COARSEN)
    return jnp.sum(grouped, axis=(1, 3, 5)) * (1.0 / COARSEN**3)


def prolong(field):
    a, b, c = field.shape
    spread = jnp.broadcast_to(
        field[:, None, :, None, :, None], (a, COARSEN, b, COARSEN, c, COARSEN)
    )
    return spread.reshape(a * COARSEN, b * COARSEN, c * COARSEN)


def shards(iterate, source, permeability, storage):
    width = MARGIN + 1
    stacked = jnp.stack([iterate, source, permeability, storage])
    margin = with_halo(stacked, (("gx", 1), ("gy", 2), ("gz", 3)), width)
    interior_region = local_subdomain_newton(
        margin[0], margin[2], margin[3][1:-1, 1:-1, 1:-1], margin[1][1:-1, 1:-1, 1:-1]
    )
    combined = interior_region[MARGIN:-MARGIN, MARGIN:-MARGIN, MARGIN:-MARGIN]
    combined_pad = with_halo(combined, (("gx", 0), ("gy", 1), ("gz", 2)), 1)
    perm_pad = margin[2][MARGIN:-MARGIN, MARGIN:-MARGIN, MARGIN:-MARGIN]
    partition_list, flow_operator, partition_weight = face_partitions(combined_pad, perm_pad, 1.0)
    fine_res = source - storage * combined + flow_operator
    coarse_base = restrict(combined)
    coarse_res = restrict(fine_res)
    coarse_perm = restrict(permeability)
    coarse_store = restrict(storage)
    inv = 1.0 / COARSEN
    coarse_pair = with_halo(
        jnp.stack([coarse_base, coarse_perm]), (("gx", 1), ("gy", 2), ("gz", 3)), 1
    )
    kcpad = coarse_pair[1]
    partition_list, flow_operator, partition_weight = face_partitions(coarse_pair[0], kcpad, inv)
    coarse_rhs = coarse_store * coarse_base - flow_operator + coarse_res
    z = coarse_base
    zpad = coarse_pair[0]
    for sweep in range(CSWEEPS):
        if sweep > 0:
            zpad = with_halo(z, (("gx", 0), ("gy", 1), ("gz", 2)), 1)
        partition_list, flow_operator, partition_weight = face_partitions(zpad, kcpad, inv)
        z = z + (coarse_rhs - coarse_store * z + flow_operator) / (coarse_store + partition_weight)
    correction = z - coarse_base
    return combined + prolong(correction)


def solution(mesh):
    in_specs = (P("gx", "gy", "gz"), P("gx", "gy", "gz"), P("gx", "gy", "gz"), P("gx", "gy", "gz"))
    out_specs = P("gx", "gy", "gz")
    return jax.shard_map(shards, mesh=mesh, in_specs=in_specs, out_specs=out_specs, check_vma=False)
```

profile of v0, /device:TPU:0, one launch (start us, length us, event | category | flops | bytes accessed | tf_op | source)
XLA Modules:
  0.0 164.0 jit_solution(4198085970892666479)
XLA Ops:
  1.0 3.0 %collective-permute-start = (f32[4,4,16,128]{3,2,1,0:T(8,128)S(1)}, f32[4,4,16,128]{3,2,1,0:T(8,128)S(1)}, u32[]{:S(2)}, u32[]{:S(2)}) collective-permute-start(f32[4,4,16,128]{3,2,1,0:T(8,128)S(1)} %get-tuple-element.87), channel_id=1, source_target_pairs={{0,16},{16,0},{1,17},{17,1},{2,18},{18,2},{3,19},{19,3},{4,20},{20... | collective-permute-start | bytes 393224 | tf_op jit(solution)/shard_map/ppermute | solution.py:20
  4.1 4.2 %collective-permute-done = f32[4,4,16,128]{3,2,1,0:T(8,128)S(1)} collective-permute-done((f32[4,4,16,128]{3,2,1,0:T(8,128)S(1)}, f32[4,4,16,128]{3,2,1,0:T(8,128)S(1)}, u32[]{:S(2)}, u32[]{:S(2)}) %collective-permute-start) | collective-permute-done | bytes 131104 | tf_op jit(solution)/shard_map/ppermute | solution.py:20
  8.3 2.0 %collective-permute-done.1 = f32[4,4,16,128]{3,2,1,0:T(8,128)S(1)} collective-permute-done((f32[4,4,16,128]{3,2,1,0:T(8,128)S(1)}, f32[4,4,16,128]{3,2,1,0:T(8,128)S(1)}, u32[]{:S(2)}, u32[]{:S(2)}) %collective-permute-start.1) | collective-permute-done | bytes 131104 | tf_op jit(solution)/shard_map/ppermute | solution.py:21
  11.5 1.8 %collective-permute-start.3 = (f32[4,16,4,128]{3,1,2,0:T(8,128)S(1)}, f32[4,16,4,128]{3,1,2,0:T(8,128)S(1)}, u32[]{:S(2)}, u32[]{:S(2)}) collective-permute-start(f32[4,16,4,128]{3,1,2,0:T(8,128)S(1)} %copy.40), channel_id=1, source_target_pairs={{4,0},{8,4},{12,8},{0,12},{5,1},{9,5},{13,9},{1,13},{6,2},{10,6},{... | collective-permute-start | bytes 393224 | tf_op jit(solution)/shard_map/ppermute | solution.py:21
  13.2 2.9 %copy.28 = f32[4,16,16,128]{2,1,3,0:T(8,128)} copy(f32[4,16,16,128]{3,2,1,0:T(8,128)S(1)} %pad_maximum_fusion.2) | data formatting | bytes 1048576 | tf_op jit(solution)/shard_map/concatenate | solution.py:22
  16.2 3.0 %copy.27 = f32[4,16,4,128]{2,1,3,0:T(8,128)} copy(f32[4,16,4,128]{3,1,2,0:T(8,128)S(1)} %collective-permute-done.2) | data formatting | bytes 262144 | tf_op jit(solution)/shard_map/ppermute | solution.py:20
  19.2 2.9 %copy.29 = f32[4,16,4,128]{2,1,3,0:T(8,128)} copy(f32[4,16,4,128]{3,1,2,0:T(8,128)S(1)} %collective-permute-done.3) | data formatting | bytes 262144 | tf_op jit(solution)/shard_map/ppermute | solution.py:21
  22.1 6.9 %pad_maximum_fusion = f32[4,16,24,128]{2,1,3,0:T(8,128)S(1)} fusion(f32[4,16,4,128]{2,1,3,0:T(8,128)} %copy.29, f32[4,16,16,128]{2,1,3,0:T(8,128)} %copy.28, f32[4,16,4,128]{2,1,3,0:T(8,128)} %copy.27), kind=kLoop, calls=%fused_computation | loop fusion | flops 393216 | bytes 1572864 | tf_op jit(solution)/shard_map/concatenate | solution.py:22
  29.0 2.0 %copy-done = f32[4,16,24,128]{2,1,3,0:T(8,128)} copy-done((f32[4,16,24,128]{2,1,3,0:T(8,128)}, f32[4,16,24,128]{2,1,3,0:T(8,128)S(1)}, u32[]{:S(2)}) %copy-start) | copy-done | bytes 786456
  31.0 1.8 %collective-permute-start.4 = (f32[4,16,24,4]{2,1,3,0:T(8,128)S(1)}, f32[4,16,24,4]{2,1,3,0:T(8,128)S(1)}, u32[]{:S(2)}, u32[]{:S(2)}) collective-permute-start(f32[4,16,24,4]{2,1,3,0:T(8,128)S(1)} %get-tuple-element.77), channel_id=1, source_target_pairs={{0,1},{1,2},{2,3},{3,0},{4,5},{5,6},{6,7},{7,4},{8,9},{9,10},{10,1... | collective-permute-start | bytes 73736 | tf_op jit(solution)/shard_map/ppermute | solution.py:20
  32.9 2.3 %collective-permute-start.5 = (f32[4,16,24,4]{2,1,3,0:T(8,128)S(1)}, f32[4,16,24,4]{2,1,3,0:T(8,128)S(1)}, u32[]{:S(2)}, u32[]{:S(2)}) collective-permute-start(f32[4,16,24,4]{2,1,3,0:T(8,128)S(1)} %get-tuple-element.78), channel_id=1, source_target_pairs={{1,0},{2,1},{3,2},{0,3},{5,4},{6,5},{7,6},{4,7},{9,8},{10,9},{11,1... | collective-permute-start | bytes 73736 | tf_op jit(solution)/shard_map/ppermute | solution.py:21
  35.1 3.0 %copy.31 = f32[4,16,24,128]{3,2,1,0:T(8,128)S(1)} copy(f32[4,16,24,128]{2,1,3,0:T(8,128)} %copy-done) | data formatting | bytes 1572864 | tf_op jit(solution)/shard_map/concatenate | solution.py:22
  45.6 9.6 %scatter.4 = f32[16,24,136]{2,1,0:T(8,128)S(1)} dynamic-update-slice(f32[16,24,136]{2,1,0:T(8,128)S(1)} %get-tuple-element.82, f32[14,22,134]{2,1,0:T(8,128)S(1)} %fusion.35, s32[]{:T(128)} %constant.33.clone.1, s32[]{:T(128)} %constant.33.clone.1, s32[]{:T(128)} %constant.33.clone.1) | dynamic-update-slice | bytes 330180 | tf_op jit(solution)/shard_map/scatter | solution.py:86
  65.4 1.8 %collective-permute-done.15 = f32[10,1,128]{2,1,0:T(1,128)S(1)} collective-permute-done((f32[10,1,128]{2,1,0:T(1,128)S(1)}, f32[10,1,128]{2,1,0:T(1,128)S(1)}, u32[]{:S(2)}, u32[]{:S(2)}) %collective-permute-start.15) | collective-permute-done | bytes 5152 | tf_op jit(solution)/shard_map/ppermute | solution.py:20
  67.3 2.8 %collective-permute-start.16 = (f32[10,18,1]{2,1,0:T(8,128)S(1)}, f32[10,18,1]{2,1,0:T(8,128)S(1)}, u32[]{:S(2)}, u32[]{:S(2)}) collective-permute-start(f32[10,18,1]{2,1,0:T(8,128)S(1)} %get-tuple-element.89), channel_id=1, source_target_pairs={{1,0},{2,1},{3,2},{0,3},{5,4},{6,5},{7,6},{4,7},{9,8},{10,9},{11,1... | collective-permute-start | bytes 2168 | tf_op jit(solution)/shard_map/ppermute | solution.py:21
  70.3 3.5 %collective-permute-done.16 = f32[10,18,1]{2,1,0:T(8,128)S(1)} collective-permute-done((f32[10,18,1]{2,1,0:T(8,128)S(1)}, f32[10,18,1]{2,1,0:T(8,128)S(1)}, u32[]{:S(2)}, u32[]{:S(2)}) %collective-permute-start.16) | collective-permute-done | bytes 752 | tf_op jit(solution)/shard_map/ppermute | solution.py:21
  73.8 3.1 %collective-permute-done.17 = f32[10,18,1]{2,1,0:T(8,128)S(1)} collective-permute-done((f32[10,18,1]{2,1,0:T(8,128)S(1)}, f32[10,18,1]{2,1,0:T(8,128)S(1)}, u32[]{:S(2)}, u32[]{:S(2)}) %collective-permute-start.17) | collective-permute-done | bytes 752 | tf_op jit(solution)/shard_map/ppermute | solution.py:20
  85.7 3.1 %collective-permute-start.11 = (f32[2,3,4,1]{3,2,1,0:T(4,128)S(1)}, f32[2,3,4,1]{3,2,1,0:T(4,128)S(1)}, u32[]{:S(2)}, u32[]{:S(2)}) collective-permute-start(f32[2,3,4,1]{3,2,1,0:T(4,128)S(1)} %get-tuple-element.96), channel_id=1, source_target_pairs={{1,0},{2,1},{3,2},{0,3},{5,4},{6,5},{7,6},{4,7},{9,8},{10,9},{11,1... | collective-permute-start | bytes 296 | tf_op jit(solution)/shard_map/ppermute | solution.py:21
  97.4 1.8 %collective-permute-done.21 = f32[3,1,16]{2,1,0:T(1,128)S(1)} collective-permute-done((f32[3,1,16]{2,1,0:T(1,128)S(1)}, f32[3,1,16]{2,1,0:T(1,128)S(1)}, u32[]{:S(2)}, u32[]{:S(2)}) %collective-permute-start.21) | collective-permute-done | bytes 224 | tf_op jit(solution)/shard_map/ppermute | solution.py:20
  99.3 3.9 %collective-permute-start.22 = (f32[3,4,1]{2,1,0:T(4,128)S(1)}, f32[3,4,1]{2,1,0:T(4,128)S(1)}, u32[]{:S(2)}, u32[]{:S(2)}) collective-permute-start(f32[3,4,1]{2,1,0:T(4,128)S(1)} %get-tuple-element.105), channel_id=1, source_target_pairs={{1,0},{2,1},{3,2},{0,3},{5,4},{6,5},{7,6},{4,7},{9,8},{10,9},{11,1... | collective-permute-start | bytes 152 | tf_op jit(solution)/shard_map/ppermute | solution.py:21
  104.6 4.1 %collective-permute-done.23 = f32[3,4,1]{2,1,0:T(4,128)S(1)} collective-permute-done((f32[3,4,1]{2,1,0:T(4,128)S(1)}, f32[3,4,1]{2,1,0:T(4,128)S(1)}, u32[]{:S(2)}, u32[]{:S(2)}) %collective-permute-start.23) | collective-permute-done | bytes 80 | tf_op jit(solution)/shard_map/ppermute | solution.py:20
  114.3 1.8 %collective-permute-done.27 = f32[3,1,16]{2,1,0:T(1,128)S(1)} collective-permute-done((f32[3,1,16]{2,1,0:T(1,128)S(1)}, f32[3,1,16]{2,1,0:T(1,128)S(1)}, u32[]{:S(2)}, u32[]{:S(2)}) %collective-permute-start.27) | collective-permute-done | bytes 224 | tf_op jit(solution)/shard_map/ppermute | solution.py:20
  116.2 2.0 %collective-permute-start.29 = (f32[3,4,1]{2,1,0:T(4,128)S(1)}, f32[3,4,1]{2,1,0:T(4,128)S(1)}, u32[]{:S(2)}, u32[]{:S(2)}) collective-permute-start(f32[3,4,1]{2,1,0:T(4,128)S(1)} %get-tuple-element.104), channel_id=1, source_target_pairs={{0,1},{1,2},{2,3},{3,0},{4,5},{5,6},{6,7},{7,4},{8,9},{9,10},{10,1... | collective-permute-start | bytes 152 | tf_op jit(solution)/shard_map/ppermute | solution.py:20
  119.8 1.9 %collective-permute-done.29 = f32[3,4,1]{2,1,0:T(4,128)S(1)} collective-permute-done((f32[3,4,1]{2,1,0:T(4,128)S(1)}, f32[3,4,1]{2,1,0:T(4,128)S(1)}, u32[]{:S(2)}, u32[]{:S(2)}) %collective-permute-start.29) | collective-permute-done | bytes 80 | tf_op jit(solution)/shard_map/ppermute | solution.py:20
  128.4 1.8 %collective-permute-done.33 = f32[3,1,16]{2,1,0:T(1,128)S(1)} collective-permute-done((f32[3,1,16]{2,1,0:T(1,128)S(1)}, f32[3,1,16]{2,1,0:T(1,128)S(1)}, u32[]{:S(2)}, u32[]{:S(2)}) %collective-permute-start.33) | collective-permute-done | bytes 224 | tf_op jit(solution)/shard_map/ppermute | solution.py:20
  130.3 2.0 %collective-permute-start.35 = (f32[3,4,1]{2,1,0:T(4,128)S(1)}, f32[3,4,1]{2,1,0:T(4,128)S(1)}, u32[]{:S(2)}, u32[]{:S(2)}) collective-permute-start(f32[3,4,1]{2,1,0:T(4,128)S(1)} %get-tuple-element.102), channel_id=1, source_target_pairs={{0,1},{1,2},{2,3},{3,0},{4,5},{5,6},{6,7},{7,4},{8,9},{9,10},{10,1... | collective-permute-start | bytes 152 | tf_op jit(solution)/shard_map/ppermute | solution.py:20
  133.9 1.9 %collective-permute-done.35 = f32[3,4,1]{2,1,0:T(4,128)S(1)} collective-permute-done((f32[3,4,1]{2,1,0:T(4,128)S(1)}, f32[3,4,1]{2,1,0:T(4,128)S(1)}, u32[]{:S(2)}, u32[]{:S(2)}) %collective-permute-start.35) | collective-permute-done | bytes 80 | tf_op jit(solution)/shard_map/ppermute | solution.py:20
  141.4 1.8 %collective-permute-done.39 = f32[3,1,16]{2,1,0:T(1,128)S(1)} collective-permute-done((f32[3,1,16]{2,1,0:T(1,128)S(1)}, f32[3,1,16]{2,1,0:T(1,128)S(1)}, u32[]{:S(2)}, u32[]{:S(2)}) %collective-permute-start.39) | collective-permute-done | bytes 224 | tf_op jit(solution)/shard_map/ppermute | solution.py:20
  143.3 2.0 %collective-permute-start.41 = (f32[3,4,1]{2,1,0:T(4,128)S(1)}, f32[3,4,1]{2,1,0:T(4,128)S(1)}, u32[]{:S(2)}, u32[]{:S(2)}) collective-permute-start(f32[3,4,1]{2,1,0:T(4,128)S(1)} %get-tuple-element.100), channel_id=1, source_target_pairs={{0,1},{1,2},{2,3},{3,0},{4,5},{5,6},{6,7},{7,4},{8,9},{9,10},{10,1... | collective-permute-start | bytes 152 | tf_op jit(solution)/shard_map/ppermute | solution.py:20
  147.0 1.9 %collective-permute-done.41 = f32[3,4,1]{2,1,0:T(4,128)S(1)} collective-permute-done((f32[3,4,1]{2,1,0:T(4,128)S(1)}, f32[3,4,1]{2,1,0:T(4,128)S(1)}, u32[]{:S(2)}, u32[]{:S(2)}) %collective-permute-start.41) | collective-permute-done | bytes 80 | tf_op jit(solution)/shard_map/ppermute | solution.py:20
  157.4 2.0 %collective-permute-start.47 = (f32[3,4,1]{2,1,0:T(4,128)S(1)}, f32[3,4,1]{2,1,0:T(4,128)S(1)}, u32[]{:S(2)}, u32[]{:S(2)}) collective-permute-start(f32[3,4,1]{2,1,0:T(4,128)S(1)} %get-tuple-element.98), channel_id=1, source_target_pairs={{0,1},{1,2},{2,3},{3,0},{4,5},{5,6},{6,7},{7,4},{8,9},{9,10},{10,1... | collective-permute-start | bytes 152 | tf_op jit(solution)/shard_map/ppermute | solution.py:20
  161.0 1.9 %collective-permute-done.47 = f32[3,4,1]{2,1,0:T(4,128)S(1)} collective-permute-done((f32[3,4,1]{2,1,0:T(4,128)S(1)}, f32[3,4,1]{2,1,0:T(4,128)S(1)}, u32[]{:S(2)}, u32[]{:S(2)}) %collective-permute-start.47) | collective-permute-done | bytes 80 | tf_op jit(solution)/shard_map/ppermute | solution.py:20
  (186 shorter events, 73.2 us)
Async XLA Ops:
  1.0 7.4 %collective-permute-start = (f32[4,4,16,128]{3,2,1,0:T(8,128)S(1)}, f32[4,4,16,128]{3,2,1,0:T(8,128)S(1)}, u32[]{:S(2)}, u32[]{:S(2)}) collective-permute-start(f32[4,4,16,128]{3,2,1,0:T(8,128)S(1)} %get-tuple-element.87), channel_id=1, source_target_pairs={{0,16},{16,0},{1,17},{17,1},{2,18},{18,2},{3,19},{19,3},{4,20},{20... | collective-permute-start | bytes 393224 | tf_op jit(solution)/shard_map/ppermute | solution.py:20
  4.0 6.3 %collective-permute-start.1 = (f32[4,4,16,128]{3,2,1,0:T(8,128)S(1)}, f32[4,4,16,128]{3,2,1,0:T(8,128)S(1)}, u32[]{:S(2)}, u32[]{:S(2)}) collective-permute-start(f32[4,4,16,128]{3,2,1,0:T(8,128)S(1)} %get-tuple-element.88), channel_id=1, source_target_pairs={{16,0},{0,16},{17,1},{1,17},{18,2},{2,18},{19,3},{3,19},{20,4},{4,... | collective-permute-start | bytes 393224 | tf_op jit(solution)/shard_map/ppermute | solution.py:21
  11.4 4.8 %collective-permute-start.2 = (f32[4,16,4,128]{3,1,2,0:T(8,128)S(1)}, f32[4,16,4,128]{3,1,2,0:T(8,128)S(1)}, u32[]{:S(2)}, u32[]{:S(2)}) collective-permute-start(f32[4,16,4,128]{3,1,2,0:T(8,128)S(1)} %copy.39), channel_id=1, source_target_pairs={{0,4},{4,8},{8,12},{12,0},{1,5},{5,9},{9,13},{13,1},{2,6},{6,10},{... | collective-permute-start | bytes 393224 | tf_op jit(solution)/shard_map/ppermute | solution.py:20
  11.5 7.7 %collective-permute-start.3 = (f32[4,16,4,128]{3,1,2,0:T(8,128)S(1)}, f32[4,16,4,128]{3,1,2,0:T(8,128)S(1)}, u32[]{:S(2)}, u32[]{:S(2)}) collective-permute-start(f32[4,16,4,128]{3,1,2,0:T(8,128)S(1)} %copy.40), channel_id=1, source_target_pairs={{4,0},{8,4},{12,8},{0,12},{5,1},{9,5},{13,9},{1,13},{6,2},{10,6},{... | collective-permute-start | bytes 393224 | tf_op jit(solution)/shard_map/ppermute | solution.py:21
  31.0 8.2 %collective-permute-start.4 = (f32[4,16,24,4]{2,1,3,0:T(8,128)S(1)}, f32[4,16,24,4]{2,1,3,0:T(8,128)S(1)}, u32[]{:S(2)}, u32[]{:S(2)}) collective-permute-start(f32[4,16,24,4]{2,1,3,0:T(8,128)S(1)} %get-tuple-element.77), channel_id=1, source_target_pairs={{0,1},{1,2},{2,3},{3,0},{4,5},{5,6},{6,7},{7,4},{8,9},{9,10},{10,1... | collective-permute-start | bytes 73736 | tf_op jit(solution)/shard_map/ppermute | solution.py:20
  32.9 7.8 %collective-permute-start.5 = (f32[4,16,24,4]{2,1,3,0:T(8,128)S(1)}, f32[4,16,24,4]{2,1,3,0:T(8,128)S(1)}, u32[]{:S(2)}, u32[]{:S(2)}) collective-permute-start(f32[4,16,24,4]{2,1,3,0:T(8,128)S(1)} %get-tuple-element.78), channel_id=1, source_target_pairs={{1,0},{2,1},{3,2},{0,3},{5,4},{6,5},{7,6},{4,7},{9,8},{10,9},{11,1... | collective-permute-start | bytes 73736 | tf_op jit(solution)/shard_map/ppermute | solution.py:21
  58.8 3.7 %collective-permute-start.12 = (f32[1,16,128]{2,1,0:T(8,128)S(1)}, f32[1,16,128]{2,1,0:T(8,128)S(1)}, u32[]{:S(2)}, u32[]{:S(2)}) collective-permute-start(f32[1,16,128]{2,1,0:T(8,128)S(1)} %get-tuple-element.86), channel_id=1, source_target_pairs={{16,0},{0,16},{17,1},{1,17},{18,2},{2,18},{19,3},{3,19},{20,4},{4,... | collective-permute-start | bytes 24584 | tf_op jit(solution)/shard_map/ppermute | solution.py:21
  60.4 3.7 %collective-permute-start.13 = (f32[1,16,128]{2,1,0:T(8,128)S(1)}, f32[1,16,128]{2,1,0:T(8,128)S(1)}, u32[]{:S(2)}, u32[]{:S(2)}) collective-permute-start(f32[1,16,128]{2,1,0:T(8,128)S(1)} %get-tuple-element.85), channel_id=1, source_target_pairs={{0,16},{16,0},{1,17},{17,1},{2,18},{18,2},{3,19},{19,3},{4,20},{20... | collective-permute-start | bytes 24584 | tf_op jit(solution)/shard_map/ppermute | solution.py:20
  67.3 6.4 %collective-permute-start.16 = (f32[10,18,1]{2,1,0:T(8,128)S(1)}, f32[10,18,1]{2,1,0:T(8,128)S(1)}, u32[]{:S(2)}, u32[]{:S(2)}) collective-permute-start(f32[10,18,1]{2,1,0:T(8,128)S(1)} %get-tuple-element.89), channel_id=1, source_target_pairs={{1,0},{2,1},{3,2},{0,3},{5,4},{6,5},{7,6},{4,7},{9,8},{10,9},{11,1... | collective-permute-start | bytes 2168 | tf_op jit(solution)/shard_map/ppermute | solution.py:21
  70.1 6.7 %collective-permute-start.17 = (f32[10,18,1]{2,1,0:T(8,128)S(1)}, f32[10,18,1]{2,1,0:T(8,128)S(1)}, u32[]{:S(2)}, u32[]{:S(2)}) collective-permute-start(f32[10,18,1]{2,1,0:T(8,128)S(1)} %get-tuple-element.90), channel_id=1, source_target_pairs={{0,1},{1,2},{2,3},{3,0},{4,5},{5,6},{6,7},{7,4},{8,9},{9,10},{10,1... | collective-permute-start | bytes 2168 | tf_op jit(solution)/shard_map/ppermute | solution.py:20
  77.4 3.7 %collective-permute-start.6 = (f32[2,1,2,16]{3,2,1,0:T(2,128)S(1)}, f32[2,1,2,16]{3,2,1,0:T(2,128)S(1)}, u32[]{:S(2)}, u32[]{:S(2)}) collective-permute-start(f32[2,1,2,16]{3,2,1,0:T(2,128)S(1)} %pad_maximum_fusion.67), channel_id=1, source_target_pairs={{0,16},{16,0},{1,17},{17,1},{2,18},{18,2},{3,19},{19,3},{4,20},{20... | collective-permute-start | bytes 776 | tf_op jit(solution)/shard_map/ppermute | solution.py:20
  78.0 3.6 %collective-permute-start.7 = (f32[2,1,2,16]{3,2,1,0:T(2,128)S(1)}, f32[2,1,2,16]{3,2,1,0:T(2,128)S(1)}, u32[]{:S(2)}, u32[]{:S(2)}) collective-permute-start(f32[2,1,2,16]{3,2,1,0:T(2,128)S(1)} %pad_maximum_fusion.67), channel_id=1, source_target_pairs={{16,0},{0,16},{17,1},{1,17},{18,2},{2,18},{19,3},{3,19},{20,4},{4,... | collective-permute-start | bytes 776 | tf_op jit(solution)/shard_map/ppermute | solution.py:21
  84.8 5.7 %collective-permute-start.10 = (f32[2,3,4,1]{3,2,1,0:T(4,128)S(1)}, f32[2,3,4,1]{3,2,1,0:T(4,128)S(1)}, u32[]{:S(2)}, u32[]{:S(2)}) collective-permute-start(f32[2,3,4,1]{3,2,1,0:T(4,128)S(1)} %get-tuple-element.95), channel_id=1, source_target_pairs={{0,1},{1,2},{2,3},{3,0},{4,5},{5,6},{6,7},{7,4},{8,9},{9,10},{10,1... | collective-permute-start | bytes 296 | tf_op jit(solution)/shard_map/ppermute | solution.py:20
  85.7 4.8 %collective-permute-start.11 = (f32[2,3,4,1]{3,2,1,0:T(4,128)S(1)}, f32[2,3,4,1]{3,2,1,0:T(4,128)S(1)}, u32[]{:S(2)}, u32[]{:S(2)}) collective-permute-start(f32[2,3,4,1]{3,2,1,0:T(4,128)S(1)} %get-tuple-element.96), channel_id=1, source_target_pairs={{1,0},{2,1},{3,2},{0,3},{5,4},{6,5},{7,6},{4,7},{9,8},{10,9},{11,1... | collective-permute-start | bytes 296 | tf_op jit(solution)/shard_map/ppermute | solution.py:21
  91.0 3.6 %collective-permute-start.18 = (f32[1,2,16]{2,1,0:T(2,128)S(1)}, f32[1,2,16]{2,1,0:T(2,128)S(1)}, u32[]{:S(2)}, u32[]{:S(2)}) collective-permute-start(f32[1,2,16]{2,1,0:T(2,128)S(1)} %get-tuple-element.50), channel_id=1, source_target_pairs={{16,0},{0,16},{17,1},{1,17},{18,2},{2,18},{19,3},{3,19},{20,4},{4,... | collective-permute-start | bytes 392 | tf_op jit(solution)/shard_map/ppermute | solution.py:21
  92.5 3.6 %collective-permute-start.19 = (f32[1,2,16]{2,1,0:T(2,128)S(1)}, f32[1,2,16]{2,1,0:T(2,128)S(1)}, u32[]{:S(2)}, u32[]{:S(2)}) collective-permute-start(f32[1,2,16]{2,1,0:T(2,128)S(1)} %get-tuple-element.50), channel_id=1, source_target_pairs={{0,16},{16,0},{1,17},{17,1},{2,18},{18,2},{3,19},{19,3},{4,20},{20... | collective-permute-start | bytes 392 | tf_op jit(solution)/shard_map/ppermute | solution.py:20
  99.3 5.2 %collective-permute-start.22 = (f32[3,4,1]{2,1,0:T(4,128)S(1)}, f32[3,4,1]{2,1,0:T(4,128)S(1)}, u32[]{:S(2)}, u32[]{:S(2)}) collective-permute-start(f32[3,4,1]{2,1,0:T(4,128)S(1)} %get-tuple-element.105), channel_id=1, source_target_pairs={{1,0},{2,1},{3,2},{0,3},{5,4},{6,5},{7,6},{4,7},{9,8},{10,9},{11,1... | collective-permute-start | bytes 152 | tf_op jit(solution)/shard_map/ppermute | solution.py:21
  103.2 5.4 %collective-permute-start.23 = (f32[3,4,1]{2,1,0:T(4,128)S(1)}, f32[3,4,1]{2,1,0:T(4,128)S(1)}, u32[]{:S(2)}, u32[]{:S(2)}) collective-permute-start(f32[3,4,1]{2,1,0:T(4,128)S(1)} %get-tuple-element.106), channel_id=1, source_target_pairs={{0,1},{1,2},{2,3},{3,0},{4,5},{5,6},{6,7},{7,4},{8,9},{9,10},{10,1... | collective-permute-start | bytes 152 | tf_op jit(solution)/shard_map/ppermute | solution.py:20
  108.8 3.6 %collective-permute-start.24 = (f32[1,2,16]{2,1,0:T(2,128)S(1)}, f32[1,2,16]{2,1,0:T(2,128)S(1)}, u32[]{:S(2)}, u32[]{:S(2)}) collective-permute-start(f32[1,2,16]{2,1,0:T(2,128)S(1)} %divide_add_fusion.3), channel_id=1, source_target_pairs={{16,0},{0,16},{17,1},{1,17},{18,2},{2,18},{19,3},{3,19},{20,4},{4,... | collective-permute-start | bytes 392 | tf_op jit(solution)/shard_map/ppermute | solution.py:21
  109.4 3.6 %collective-permute-start.25 = (f32[1,2,16]{2,1,0:T(2,128)S(1)}, f32[1,2,16]{2,1,0:T(2,128)S(1)}, u32[]{:S(2)}, u32[]{:S(2)}) collective-permute-start(f32[1,2,16]{2,1,0:T(2,128)S(1)} %divide_add_fusion.3), channel_id=1, source_target_pairs={{0,16},{16,0},{1,17},{17,1},{2,18},{18,2},{3,19},{19,3},{4,20},{20... | collective-permute-start | bytes 392 | tf_op jit(solution)/shard_map/ppermute | solution.py:20
  116.2 3.6 %collective-permute-start.28 = (f32[3,4,1]{2,1,0:T(4,128)S(1)}, f32[3,4,1]{2,1,0:T(4,128)S(1)}, u32[]{:S(2)}, u32[]{:S(2)}) collective-permute-start(f32[3,4,1]{2,1,0:T(4,128)S(1)} %get-tuple-element.103), channel_id=1, source_target_pairs={{1,0},{2,1},{3,2},{0,3},{5,4},{6,5},{7,6},{4,7},{9,8},{10,9},{11,1... | collective-permute-start | bytes 152 | tf_op jit(solution)/shard_map/ppermute | solution.py:21
  116.2 5.5 %collective-permute-start.29 = (f32[3,4,1]{2,1,0:T(4,128)S(1)}, f32[3,4,1]{2,1,0:T(4,128)S(1)}, u32[]{:S(2)}, u32[]{:S(2)}) collective-permute-start(f32[3,4,1]{2,1,0:T(4,128)S(1)} %get-tuple-element.104), channel_id=1, source_target_pairs={{0,1},{1,2},{2,3},{3,0},{4,5},{5,6},{6,7},{7,4},{8,9},{9,10},{10,1... | collective-permute-start | bytes 152 | tf_op jit(solution)/shard_map/ppermute | solution.py:20
  121.9 3.6 %collective-permute-start.30 = (f32[1,2,16]{2,1,0:T(2,128)S(1)}, f32[1,2,16]{2,1,0:T(2,128)S(1)}, u32[]{:S(2)}, u32[]{:S(2)}) collective-permute-start(f32[1,2,16]{2,1,0:T(2,128)S(1)} %divide_add_fusion.2), channel_id=1, source_target_pairs={{16,0},{0,16},{17,1},{1,17},{18,2},{2,18},{19,3},{3,19},{20,4},{4,... | collective-permute-start | bytes 392 | tf_op jit(solution)/shard_map/ppermute | solution.py:21
  123.4 3.6 %collective-permute-start.31 = (f32[1,2,16]{2,1,0:T(2,128)S(1)}, f32[1,2,16]{2,1,0:T(2,128)S(1)}, u32[]{:S(2)}, u32[]{:S(2)}) collective-permute-start(f32[1,2,16]{2,1,0:T(2,128)S(1)} %divide_add_fusion.2), channel_id=1, source_target_pairs={{0,16},{16,0},{1,17},{17,1},{2,18},{18,2},{3,19},{19,3},{4,20},{20... | collective-permute-start | bytes 392 | tf_op jit(solution)/shard_map/ppermute | solution.py:20
  130.3 3.6 %collective-permute-start.34 = (f32[3,4,1]{2,1,0:T(4,128)S(1)}, f32[3,4,1]{2,1,0:T(4,128)S(1)}, u32[]{:S(2)}, u32[]{:S(2)}) collective-permute-start(f32[3,4,1]{2,1,0:T(4,128)S(1)} %get-tuple-element.101), channel_id=1, source_target_pairs={{1,0},{2,1},{3,2},{0,3},{5,4},{6,5},{7,6},{4,7},{9,8},{10,9},{11,1... | collective-permute-start | bytes 152 | tf_op jit(solution)/shard_map/ppermute | solution.py:21
  130.3 5.5 %collective-permute-start.35 = (f32[3,4,1]{2,1,0:T(4,128)S(1)}, f32[3,4,1]{2,1,0:T(4,128)S(1)}, u32[]{:S(2)}, u32[]{:S(2)}) collective-permute-start(f32[3,4,1]{2,1,0:T(4,128)S(1)} %get-tuple-element.102), channel_id=1, source_target_pairs={{0,1},{1,2},{2,3},{3,0},{4,5},{5,6},{6,7},{7,4},{8,9},{9,10},{10,1... | collective-permute-start | bytes 152 | tf_op jit(solution)/shard_map/ppermute | solution.py:20
  136.0 3.6 %collective-permute-start.36 = (f32[1,2,16]{2,1,0:T(2,128)S(1)}, f32[1,2,16]{2,1,0:T(2,128)S(1)}, u32[]{:S(2)}, u32[]{:S(2)}) collective-permute-start(f32[1,2,16]{2,1,0:T(2,128)S(1)} %divide_add_fusion.1), channel_id=1, source_target_pairs={{16,0},{0,16},{17,1},{1,17},{18,2},{2,18},{19,3},{3,19},{20,4},{4,... | collective-permute-start | bytes 392 | tf_op jit(solution)/shard_map/ppermute | solution.py:21
  143.3 3.6 %collective-permute-start.40 = (f32[3,4,1]{2,1,0:T(4,128)S(1)}, f32[3,4,1]{2,1,0:T(4,128)S(1)}, u32[]{:S(2)}, u32[]{:S(2)}) collective-permute-start(f32[3,4,1]{2,1,0:T(4,128)S(1)} %get-tuple-element.99), channel_id=1, source_target_pairs={{1,0},{2,1},{3,2},{0,3},{5,4},{6,5},{7,6},{4,7},{9,8},{10,9},{11,1... | collective-permute-start | bytes 152 | tf_op jit(solution)/shard_map/ppermute | solution.py:21
  143.3 5.5 %collective-permute-start.41 = (f32[3,4,1]{2,1,0:T(4,128)S(1)}, f32[3,4,1]{2,1,0:T(4,128)S(1)}, u32[]{:S(2)}, u32[]{:S(2)}) collective-permute-start(f32[3,4,1]{2,1,0:T(4,128)S(1)} %get-tuple-element.100), channel_id=1, source_target_pairs={{0,1},{1,2},{2,3},{3,0},{4,5},{5,6},{6,7},{7,4},{8,9},{9,10},{10,1... | collective-permute-start | bytes 152 | tf_op jit(solution)/shard_map/ppermute | solution.py:20
  149.0 3.6 %collective-permute-start.42 = (f32[1,2,16]{2,1,0:T(2,128)S(1)}, f32[1,2,16]{2,1,0:T(2,128)S(1)}, u32[]{:S(2)}, u32[]{:S(2)}) collective-permute-start(f32[1,2,16]{2,1,0:T(2,128)S(1)} %divide_add_fusion), channel_id=1, source_target_pairs={{16,0},{0,16},{17,1},{1,17},{18,2},{2,18},{19,3},{3,19},{20,4},{4,... | collective-permute-start | bytes 392 | tf_op jit(solution)/shard_map/ppermute | solution.py:21
  157.4 3.6 %collective-permute-start.46 = (f32[3,4,1]{2,1,0:T(4,128)S(1)}, f32[3,4,1]{2,1,0:T(4,128)S(1)}, u32[]{:S(2)}, u32[]{:S(2)}) collective-permute-start(f32[3,4,1]{2,1,0:T(4,128)S(1)} %get-tuple-element.97), channel_id=1, source_target_pairs={{1,0},{2,1},{3,2},{0,3},{5,4},{6,5},{7,6},{4,7},{9,8},{10,9},{11,1... | collective-permute-start | bytes 152 | tf_op jit(solution)/shard_map/ppermute | solution.py:21
  157.4 5.5 %collective-permute-start.47 = (f32[3,4,1]{2,1,0:T(4,128)S(1)}, f32[3,4,1]{2,1,0:T(4,128)S(1)}, u32[]{:S(2)}, u32[]{:S(2)}) collective-permute-start(f32[3,4,1]{2,1,0:T(4,128)S(1)} %get-tuple-element.98), channel_id=1, source_target_pairs={{0,1},{1,2},{2,3},{3,0},{4,5},{5,6},{6,7},{7,4},{8,9},{9,10},{10,1... | collective-permute-start | bytes 152 | tf_op jit(solution)/shard_map/ppermute | solution.py:20
  (20 other events, 83.7 us)
where the time goes:
time: 164 us
  waiting for transfers between devices  70 us (43%)
  starting transfers between devices  47.3 us (29%)
  local copies, waits for them, and re-layouts  26 us (16%)
  other arithmetic  20.1 us (12%)
    ppermute x24, waiting for transfers between devices, with_halo(): before = lax.ppermute(last, axis, up)  41.6 us
    ppermute x24, waiting for transfers between devices, with_halo(): after = lax.ppermute(initial, axis, down)  28.4 us
    ppermute x24, starting transfers between devices, with_halo(): after = lax.ppermute(initial, axis, down)  24.7 us
    ppermute x24, starting transfers between devices, with_halo(): before = lax.ppermute(last, axis, up)  22.7 us
    scatter x1, local copies, waits for them, and re-layouts, local_subdomain_newton(): value_padded = value_padded.at[1:-1, 1:-1, 1:-1].set(interior_region)  9.61 us
    concatenate x18, other arithmetic, with_halo(): x = jnp.concatenate([before, x, after], axis=dim)  8.77 us
    concatenate x2, local copies, waits for them, and re-layouts, with_halo(): x = jnp.concatenate([before, x, after], axis=dim)  5.95 us
    mul x27, other arithmetic, face_partitions(): flux = partition_list[axis] * diffs[axis]  3.75 us
  transfers between devices with their start and end apart: 48, of which 44 were waited for; matrix products, arithmetic and copies ran while one was open for 6% of the time, Pallas kernels for 0%

commit v1 on v0

v1 whole, which is shorter than its diff:
```python
import functools

import jax
import jax.numpy as jnp
from jax import lax
from jax.experimental import pallas as pl
from jax.experimental.pallas import tpu as pltpu
from jax.sharding import PartitionSpec as P

NEWTON = 2
SWEEPS = 4
CSWEEPS = 6
AXES = ("gx", "gy", "gz")
F32 = jnp.float32
ROWS = 152
FIRST = 8
LAST = 144
CHUNK = 16
ITER, SRC, PERM, STORE = 0, 1, 2, 3
ORDER = (ITER, PERM, SRC, STORE)


def g(d):
    y = d * d + 1.0
    r = lax.rsqrt(y)
    return lax.rsqrt(y * r)


def iota(shape, dim):
    return lax.broadcasted_iota(jnp.int32, shape, dim)


def roll(v, shift, axis):
    return pltpu.roll(v, shift % v.shape[axis], axis)


def y_up(tiles):
    rolled = [roll(v, -16, 1) for v in tiles]
    inside = iota(tiles[0].shape, 1) < 112
    return [jnp.where(inside, rolled[t], rolled[(t + 1) % 3]) for t in range(3)]


def y_down(tiles):
    rolled = [roll(v, 16, 1) for v in tiles]
    inside = iota(tiles[0].shape, 1) >= 16
    return [jnp.where(inside, rolled[t], rolled[(t - 1) % 3]) for t in range(3)]


def chunks():
    at = FIRST
    while at < LAST:
        size = min(CHUNK, LAST - at)
        yield at, size
        at += size


def newton(T, AX, AY, AZ, FZ, RES, RD, D):
    for it in range(NEWTON):
        for r, n in chunks():
            v = [T[ITER, t, r : r + n, :] for t in range(3)]
            k = [T[PERM, t, r : r + n, :] for t in range(3)]
            vy, ky = y_up(v), y_up(k)
            ay, fy, ax, fx = [], [], [], []
            for t in range(3):
                d = vy[t] - v[t]
                a = (0.5 * (ky[t] + k[t])) * g(d)
                AY[t, r : r + n, :] = a
                ay.append(a)
                fy.append(a * d)
                d = roll(v[t], -1, 1) - v[t]
                a = (0.5 * (roll(k[t], -1, 1) + k[t])) * g(d)
                AX[t, r : r + n, :] = a
                ax.append(a)
                fx.append(a * d)
            aym, fym = y_down(ay), y_down(fy)
            lane = iota((n, 128), 1)
            row = iota((n, 128), 0) + (r - FIRST)
            x, yl = lane % 16, lane // 16
            for t in range(3):
                d = T[ITER, t, r + 1 : r + n + 1, :] - v[t]
                az = (0.5 * (T[PERM, t, r + 1 : r + n + 1, :] + k[t])) * g(d)
                fz = az * d
                AZ[t, r : r + n, :] = az
                FZ[t, r : r + n, :] = fz
                azm = AZ[t, r - 1 : r + n - 1, :]
                fzm = FZ[t, r - 1 : r + n - 1, :]
                flow = (fz - fzm) + (fy[t] - fym[t]) + (fx[t] - roll(fx[t], 1, 1))
                weight = (az + azm) + (ay[t] + aym[t]) + (ax[t] + roll(ax[t], 1, 1))
                c = T[STORE, t, r : r + n, :]
                res = T[SRC, t, r : r + n, :] - c * v[t] + flow
                y = yl + 8 * t
                known = (x >= 1) & (x <= 14) & (y >= 1) & (y <= 22) & (row >= 1) & (row <= 134)
                rd = jnp.where(known, 1.0 / (c + weight), 0.0)
                RES[t, r : r + n, :] = res
                RD[t, r : r + n, :] = rd
                D[0, t, r : r + n, :] = res * rd
        for sweep in range(SWEEPS - 1):
            old, new = sweep % 2, (sweep + 1) % 2
            for r, n in chunks():
                d = [D[old, t, r : r + n, :] for t in range(3)]
                ay = [AY[t, r : r + n, :] for t in range(3)]
                up = y_up(d)
                down = y_down([ay[t] * d[t] for t in range(3)])
                for t in range(3):
                    ax = AX[t, r : r + n, :]
                    total = RES[t, r : r + n, :] + ay[t] * up[t] + down[t]
                    total += ax * roll(d[t], -1, 1) + roll(ax * d[t], 1, 1)
                    total += AZ[t, r : r + n, :] * D[old, t, r + 1 : r + n + 1, :]
                    total += AZ[t, r - 1 : r + n - 1, :] * D[old, t, r - 1 : r + n - 1, :]
                    delta = total * RD[t, r : r + n, :]
                    if sweep < SWEEPS - 2:
                        D[new, t, r : r + n, :] = delta
                    else:
                        T[ITER, t, r : r + n, :] = T[ITER, t, r : r + n, :] + delta


def coarse_flow(z, k, inv):
    n = len(z)
    flow, weight = [], []
    up = []
    for i in range(n):
        d = z[(i + 1) % n] - z[i]
        a = (0.5 * inv * inv * (k[(i + 1) % n] + k[i])) * g(d * inv)
        up.append((a, a * d))
    for i in range(n):
        a, f = up[i]
        am, fm = up[i - 1]
        w, fl = a + am, f - fm
        for axis in range(2):
            d = roll(z[i], -1, axis) - z[i]
            a = (0.5 * inv * inv * (roll(k[i], -1, axis) + k[i])) * g(d * inv)
            f = a * d
            w = w + (a + roll(a, 1, axis))
            fl = fl + (f - roll(f, 1, axis))
        flow.append(fl)
        weight.append(w)
    return flow, weight


def kernel(
    sizes, it_ref, src_ref, perm_ref, store_ref, out,
    I, XR, PA, T, ZS, ZR, AX, AY, AZ, FZ, RES, RD, D, Q, CB, XS, XF, YF, FS, ZF,
    GS, GZ, GM, GY, GV, GX, CR,
    lsem, xs_sem, xr_sem, ys_sem, yr_sem, zs_sem, zr_sem, fs_sem, fr_sem, gs_sem, gr_sem,
):
    nx, ny, nz = sizes
    size = dict(zip(AXES, sizes))
    me = {name: lax.axis_index(name) for name in AXES}

    def there(name, step):
        return {name: lax.rem(me[name] + (step + size[name]), size[name])}

    def send(src, dst, s, r, name, step):
        copy = pltpu.make_async_remote_copy(
            src_ref=src, dst_ref=dst, send_sem=s, recv_sem=r,
            device_id=there(name, step), device_id_type=pl.DeviceIdType.MESH,
        )
        copy.start()
        return copy

    barrier = pltpu.get_barrier_semaphore()
    for name in AXES:
        for step in range(1, size[name]):
            pl.semaphore_signal(
                barrier, inc=1, device_id=there(name, step), device_id_type=pl.DeviceIdType.MESH
            )
    local = {}
    for a, ref in enumerate((it_ref, src_ref, perm_ref, store_ref)):
        local[a] = pltpu.make_async_copy(ref, I.at[a], lsem.at[a])
        local[a].start()
    for buf in (T,):
        for a in range(4):
            for t in range(3):
                buf[a, t, 0:FIRST, :] = jnp.zeros((FIRST, 128), F32)
                buf[a, t, LAST:ROWS, :] = jnp.zeros((ROWS - LAST, 128), F32)
    for buf in (AZ, FZ):
        for t in range(3):
            buf[t, 0:FIRST, :] = jnp.zeros((FIRST, 128), F32)
    for b in range(2):
        for t in range(3):
            D[b, t, 0:FIRST, :] = jnp.zeros((FIRST, 128), F32)
            D[b, t, LAST:ROWS, :] = jnp.zeros((ROWS - LAST, 128), F32)
    for a in range(4):
        local[a].wait()
    pl.semaphore_wait(barrier, nx + ny + nz - 3)

    sent = []
    xcopy, ycopy, zcopy = {}, {}, {}
    for a in ORDER:
        hi = send(I.at[a, pl.ds(64, 64)], XR.at[a, 0], xs_sem.at[2 * a], xr_sem.at[2 * a], "gx", 1)
        lo = send(I.at[a, pl.ds(0, 64)], XR.at[a, 1], xs_sem.at[2 * a + 1], xr_sem.at[2 * a + 1], "gx", -1)
        xcopy[a] = (hi, lo)
        sent += [hi, lo]
    for a in ORDER:
        for x in range(8):
            PA[a, pl.ds(64 + 4 + x, 16, stride=16), :] = I[a, 16 * x : 16 * x + 16, :]
    for a in ORDER:
        for side in range(2):
            xcopy[a][side].wait_recv()
            for x in range(4):
                PA[a, pl.ds(64 + 12 * side + x, 16, stride=16), :] = XR[a, side, 16 * x : 16 * x + 16, :]
        hi = send(PA.at[a, pl.ds(256, 64)], PA.at[a, pl.ds(0, 64)], ys_sem.at[2 * a], yr_sem.at[2 * a], "gy", 1)
        lo = send(PA.at[a, pl.ds(64, 64)], PA.at[a, pl.ds(320, 64)], ys_sem.at[2 * a + 1], yr_sem.at[2 * a + 1], "gy", -1)
        ycopy[a] = (hi, lo)
        sent += [hi, lo]
    for p in range(2):
        for h in range(2):
            a = ORDER[2 * p + h]
            ycopy[a][0].wait_recv()
            ycopy[a][1].wait_recv()
            for t in range(3):
                m = PA[a, 128 * t : 128 * t + 128, :].T
                T[a, t, 12:140, :] = m
                ZS[p, 0, t, 4 * h : 4 * h + 4, :] = m[124:128, :]
                ZS[p, 1, t, 4 * h : 4 * h + 4, :] = m[0:4, :]
        hi = send(ZS.at[p, 0], ZR.at[p, 0], zs_sem.at[2 * p], zr_sem.at[2 * p], "gz", 1)
        lo = send(ZS.at[p, 1], ZR.at[p, 1], zs_sem.at[2 * p + 1], zr_sem.at[2 * p + 1], "gz", -1)
        zcopy[p] = (hi, lo)
        sent += [hi, lo]
    for p in range(2):
        zcopy[p][0].wait_recv()
        zcopy[p][1].wait_recv()
        for h in range(2):
            a = ORDER[2 * p + h]
            for t in range(3):
                T[a, t, 8:12, :] = ZR[p, 0, t, 4 * h : 4 * h + 4, :]
                T[a, t, 140:144, :] = ZR[p, 1, t, 4 * h : 4 * h + 4, :]

    newton(T, AX, AY, AZ, FZ, RES, RD, D)

    for t in range(3):
        Q[128 * t : 128 * t + 128, :] = T[ITER, t, 12:140, :].T
    lane = iota((8, 128), 1)
    pack_c = jnp.zeros((8, 128), F32)
    pack_k = jnp.zeros((8, 128), F32)
    for y in range(16):
        b = (y + 4) * 16 + 4
        c = Q[b : b + 8, :]
        CB[8 * y : 8 * y + 8, :] = c
        pack_c = jnp.where(lane // 2 == y, roll(c, 1 + 2 * y, 1), pack_c)
        pack_k = jnp.where(lane // 2 == y, roll(PA[PERM, b : b + 8, :], 1 + 2 * y, 1), pack_k)
    XS[0, :, :] = Q[pl.ds(64 + 11, 16, stride=16), :]
    XS[1, :, :] = Q[pl.ds(64 + 4, 16, stride=16), :]
    FS[0:8, :] = pack_c
    FS[8:16, :] = pack_k
    faces = [
        send(XS.at[0], XF.at[0], fs_sem.at[0], fr_sem.at[0], "gx", 1),
        send(XS.at[1], XF.at[1], fs_sem.at[1], fr_sem.at[1], "gx", -1),
        send(CB.at[pl.ds(120, 8)], YF.at[0], fs_sem.at[2], fr_sem.at[2], "gy", 1),
        send(CB.at[pl.ds(0, 8)], YF.at[1], fs_sem.at[3], fr_sem.at[3], "gy", -1),
        send(FS, ZF.at[0], fs_sem.at[4], fr_sem.at[4], "gz", 1),
        send(FS, ZF.at[1], fs_sem.at[5], fr_sem.at[5], "gz", -1),
    ]
    sent += faces
    for copy in faces:
        copy.wait_recv()
    Q[pl.ds(64 + 3, 16, stride=16), :] = XF[0, :, :]
    Q[pl.ds(64 + 12, 16, stride=16), :] = XF[1, :, :]
    Q[3 * 16 + 4 : 3 * 16 + 12, :] = YF[0, :, :]
    Q[20 * 16 + 4 : 20 * 16 + 12, :] = YF[1, :, :]

    sums = [[None, None] for _ in range(4)]

    def add(q, j, value):
        sums[q][j] = value if sums[q][j] is None else sums[q][j] + value

    zf = [ZF[0, 0:8, :], ZF[1, 0:8, :]]
    zk = [ZF[0, 8:16, :], ZF[1, 8:16, :]]
    for y in range(16):
        b = (y + 4) * 16 + 4
        c, k = Q[b : b + 8, :], PA[PERM, b : b + 8, :]
        near = [(Q[b + o : b + o + 8, :], PA[PERM, b + o : b + o + 8, :]) for o in (1, -1, 16, -16)]
        near.append(tuple(
            jnp.where(lane == 127, roll(far, 126 - 2 * y, 1), roll(own, -1, 1))
            for far, own in ((zf[1], c), (zk[1], k))
        ))
        near.append(tuple(
            jnp.where(lane == 0, roll(far, -2 * y, 1), roll(own, 1, 1))
            for far, own in ((zf[0], c), (zk[0], k))
        ))
        flow = 0.0
        for cn, kn in near:
            d = cn - c
            flow = flow + (0.5 * (k + kn)) * g(d) * d
        st = PA[STORE, b : b + 8, :]
        j = y // 8
        add(0, j, c)
        add(1, j, PA[SRC, b : b + 8, :] - st * c + flow)
        add(2, j, k)
        add(3, j, st)
    rows = [jnp.sum(sums[q][j], axis=0, keepdims=True) for q in range(4) for j in range(2)]
    mean = jnp.where(iota((128, 128), 0) // 8 == iota((128, 128), 1) % 16, 1.0 / 512, 0.0).astype(F32)
    tile = jnp.dot(
        jnp.concatenate(rows, axis=0), mean,
        precision=lax.Precision.HIGHEST, preferred_element_type=F32,
    )

    width = GM.shape[-1]

    def gather(src, buf, name, base):
        n = size[name]
        copies = [
            send(src, buf.at[me[name]], gs_sem.at[base + s - 1], gr_sem.at[base + s - 1], name, s)
            for s in range(1, n)
        ]
        buf[me[name]] = src[...]
        for copy in copies:
            copy.wait_recv()
        sent.extend(copies)

    GS[...] = tile
    gather(GS, GZ, "gz", 0)
    wlane = iota((8, width), 1)
    merged = None
    for z in range(nz):
        part = GZ[z]
        if width > 128:
            part = jnp.concatenate([part] * (width // 128), axis=1)
        merged = part if merged is None else jnp.where((wlane // 16) % nz == z, part, merged)
    GM[...] = merged
    gather(GM, GY, "gy", nz - 1)
    for y in range(ny):
        for q in range(4):
            GV[8 * q + 2 * y : 8 * q + 2 * y + 2, :] = GY[y, 2 * q : 2 * q + 2, :]
    gather(GV, GX, "gx", nz + ny - 2)

    base = [GX[i, 0:8, :] for i in range(nx)]
    cres = [GX[i, 8:16, :] for i in range(nx)]
    kc = [GX[i, 16:24, :] for i in range(nx)]
    sc = [GX[i, 24:32, :] for i in range(nx)]
    flow, weight = coarse_flow(base, kc, 1.0 / 8)
    rhs = [sc[i] * base[i] - flow[i] + cres[i] for i in range(nx)]
    z = [base[i] + cres[i] / (sc[i] + weight[i]) for i in range(nx)]
    for sweep in range(1, CSWEEPS):
        flow, weight = coarse_flow(z, kc, 1.0 / 8)
        z = [z[i] + (rhs[i] - sc[i] * z[i] + flow[i]) / (sc[i] + weight[i]) for i in range(nx)]
    for i in range(nx):
        CR[i, :, :] = z[i] - base[i]
    spread = jnp.where(
        iota((width, 128), 0) == 16 * me["gz"] + iota((width, 128), 1) // 8, 1.0, 0.0
    ).astype(F32)
    wide = jnp.dot(
        CR[me["gx"]], spread, precision=lax.Precision.HIGHEST, preferred_element_type=F32
    )
    sub = iota((8, 128), 0)
    for j in range(2):
        line = jnp.sum(jnp.where(sub == 2 * me["gy"] + j, wide, 0.0), axis=0, keepdims=True)
        for y in range(8 * j, 8 * j + 8):
            out[pl.ds(y, 8, stride=16), :] = CB[8 * y : 8 * y + 8, :] + line
    for copy in sent:
        copy.wait_send()


def shards(sizes, *args):
    nx, ny, nz = sizes
    width = max(128, 16 * nz)
    field = lambda *lead: pltpu.VMEM(lead + (3, ROWS, 128), F32)
    links = nx + ny + nz - 3
    scratch = [
        pltpu.VMEM((4, 128, 128), F32),
        pltpu.VMEM((4, 2, 64, 128), F32),
        pltpu.VMEM((4, 384, 128), F32),
        field(4),
        pltpu.VMEM((2, 2, 3, 8, 128), F32),
        pltpu.VMEM((2, 2, 3, 8, 128), F32),
        field(), field(), field(), field(), field(), field(), field(2),
        pltpu.VMEM((384, 128), F32),
        pltpu.VMEM((128, 128), F32),
        pltpu.VMEM((2, 16, 128), F32),
        pltpu.VMEM((2, 16, 128), F32),
        pltpu.VMEM((2, 8, 128), F32),
        pltpu.VMEM((16, 128), F32),
        pltpu.VMEM((2, 16, 128), F32),
        pltpu.VMEM((8, 128), F32),
        pltpu.VMEM((nz, 8, 128), F32),
        pltpu.VMEM((8, width), F32),
        pltpu.VMEM((ny, 8, width), F32),
        pltpu.VMEM((32, width), F32),
        pltpu.VMEM((nx, 32, width), F32),
        pltpu.VMEM((nx, 8, width), F32),
    ] + [pltpu.SemaphoreType.DMA((n,)) for n in (4, 8, 8, 8, 8, 4, 4, 6, 6, links, links)]
    out = pl.pallas_call(
        functools.partial(kernel, sizes),
        out_shape=jax.ShapeDtypeStruct((128, 128), F32),
        in_specs=[pl.BlockSpec(memory_space=pl.ANY)] * 4,
        out_specs=pl.BlockSpec(memory_space=pltpu.VMEM),
        scratch_shapes=scratch,
        compiler_params=pltpu.CompilerParams(
            collective_id=0, has_side_effects=True, vmem_limit_bytes=24 * 1024 * 1024
        ),
    )(*[x.reshape(128, 128) for x in args])
    return out.reshape(8, 16, 128)


def solution(mesh):
    spec = P(*AXES)
    sizes = tuple(mesh.shape[name] for name in AXES)
    return jax.shard_map(
        functools.partial(shards, sizes), mesh=mesh, in_specs=(spec,) * 4, out_specs=spec, check_vma=False
    )
```

time: 164 us -> 40.7 us (0.25)
  waiting for transfers between devices: 70 us -> 0 us
  starting transfers between devices: 47.3 us -> 0 us
  Pallas kernels: 0 us -> 36.4 us
  local copies, waits for them, and re-layouts: 26 us -> 3.99 us
  other arithmetic: 20.1 us -> 0 us
    ppermute x48 -> x0, waiting for transfers between devices: 70 us -> none  [the longest x24 41.6 us: with_halo(): before = lax.ppermute(last, axis, up)]
    ppermute x48 -> x0, starting transfers between devices: 47.3 us -> none  [the longest x24 24.7 us: with_halo(): after = lax.ppermute(initial, axis, down)]
    pallas_call x0 -> x1, Pallas kernels: none -> 36.4 us  [shards(): pl.pallas_call(functools.partial(kernel, sizes), out_shape=jax.ShapeDtype...]
    scatter x1 -> x0, local copies, waits for them, and re-layouts: 9.61 us -> none  [local_subdomain_newton(): value_padded = value_padded.at[1:-1, 1:-1, 1:-1].set(interior_region)]
    concatenate x18 -> x0, other arithmetic: 8.77 us -> none  [with_halo(): x = jnp.concatenate([before, x, after], axis=dim)]
    ppermute x4 -> x0, local copies, waits for them, and re-layouts: 6.87 us -> none  [the longest x2 3.48 us: with_halo(): before = lax.ppermute(last, axis, up)]
    concatenate x2 -> x0, local copies, waits for them, and re-layouts: 5.95 us -> none  [with_halo(): x = jnp.concatenate([before, x, after], axis=dim)]
    mul x38 -> x0, other arithmetic: 4.24 us -> none  [the longest x27 3.75 us: face_partitions(): flux = partition_list[axis] * diffs[axis]]
  transfers between devices with their start and end apart: 48 -> 0, of which waited for: 44 -> 0; matrix products, arithmetic and copies ran while one was open for 6% -> 0% of each run, Pallas kernels for 0% -> 0%
where the time goes in v1:
time: 40.7 us; the launch traced here: 40.4 us
  Pallas kernels  36.4 us (89%)
  local copies, waits for them, and re-layouts  3.99 us (10%)
    pallas_call x1, Pallas kernels, shards(): pl.pallas_call(functools.partial(kernel, sizes), out_shape=jax.ShapeDtype...  36.4 us
    unnamed x9, local copies, waits for them, and re-layouts  3.99 us

profile of v1, /device:TPU:0, one launch (start us, length us, event | category | flops | bytes accessed | tf_op | source)
XLA Modules:
  0.0 40.4 jit_solution(2762747157464071952)
XLA Ops:
  0.0 0.0 copy-start
  0.0 0.8 %copy-done = f32[8,16,128]{2,1,0:T(8,128)S(1)} copy-done((f32[8,16,128]{2,1,0:T(8,128)S(1)}, f32[8,16,128]{2,1,0:T(8,128)}, u32[]{:S(2)}) %copy-start) | copy-done | bytes 65560
  0.8 0.0 copy-start.1
  0.8 0.8 %copy-done.1 = f32[8,16,128]{2,1,0:T(8,128)S(1)} copy-done((f32[8,16,128]{2,1,0:T(8,128)S(1)}, f32[8,16,128]{2,1,0:T(8,128)}, u32[]{:S(2)}) %copy-start.1) | copy-done | bytes 65560
  1.7 0.0 copy-start.2
  1.7 0.8 %copy-done.2 = f32[8,16,128]{2,1,0:T(8,128)S(1)} copy-done((f32[8,16,128]{2,1,0:T(8,128)S(1)}, f32[8,16,128]{2,1,0:T(8,128)}, u32[]{:S(2)}) %copy-start.2) | copy-done | bytes 65560
  2.5 0.0 copy-start.3
  2.5 0.8 %copy-done.3 = f32[8,16,128]{2,1,0:T(8,128)S(1)} copy-done((f32[8,16,128]{2,1,0:T(8,128)S(1)}, f32[8,16,128]{2,1,0:T(8,128)}, u32[]{:S(2)}) %copy-start.3) | copy-done | bytes 65560
  3.4 36.4 %shard_map.46 = f32[128,128]{1,0:T(8,128)S(1)} custom-call(f32[128,128]{1,0:T(8,128)S(1)} %bitcast.6, f32[128,128]{1,0:T(8,128)S(1)} %bitcast.7, f32[128,128]{1,0:T(8,128)S(1)} %bitcast.8, f32[128,128]{1,0:T(8,128)S(1)} %bitcast.9), custom_call_target="tpu_custom_call" | custom-call | tf_op jit(solution)/shard_map/pallas_call | solution.py:382
  39.7 0.6 %copy.6 = f32[8,16,128]{2,1,0:T(8,128)} copy(f32[8,16,128]{2,1,0:T(8,128)S(1)} %bitcast.5) | data formatting | bytes 131072
Async XLA Ops:
  0.0 0.8 %copy-start = (f32[8,16,128]{2,1,0:T(8,128)S(1)}, f32[8,16,128]{2,1,0:T(8,128)}, u32[]{:S(2)}) copy-start(f32[8,16,128]{2,1,0:T(8,128)} %param.4) | copy-start | bytes 196612
  0.8 0.8 %copy-start.1 = (f32[8,16,128]{2,1,0:T(8,128)S(1)}, f32[8,16,128]{2,1,0:T(8,128)}, u32[]{:S(2)}) copy-start(f32[8,16,128]{2,1,0:T(8,128)} %param.5) | copy-start | bytes 196612
  1.7 0.8 %copy-start.2 = (f32[8,16,128]{2,1,0:T(8,128)S(1)}, f32[8,16,128]{2,1,0:T(8,128)}, u32[]{:S(2)}) copy-start(f32[8,16,128]{2,1,0:T(8,128)} %param.6) | copy-start | bytes 196612
  2.5 0.8 %copy-start.3 = (f32[8,16,128]{2,1,0:T(8,128)S(1)}, f32[8,16,128]{2,1,0:T(8,128)}, u32[]{:S(2)}) copy-start(f32[8,16,128]{2,1,0:T(8,128)} %param.7) | copy-start | bytes 196612

commit v2 on v1

--- a/solution.py
+++ b/solution.py
@@ -137,14 +137,21 @@
     return flow, weight
 
 
+def reaches(sizes):
+    rx, ry, rz = (n // 2 for n in sizes)
+    spare = max(rx - 1, 0) + max(ry - 1, 0) + max(rz - 1, 0)
+    return spare <= 2 and 16 * sizes[2] <= 128
+
+
 def kernel(
     sizes, it_ref, src_ref, perm_ref, store_ref, out,
     I, XR, PA, T, ZS, ZR, AX, AY, AZ, FZ, RES, RD, D, Q, CB, XS, XF, YF, FS, ZF,
-    GS, GZ, GM, GY, GV, GX, CR,
+    GS, GA, GZ, GM, GY, GV, GX, CR,
     lsem, xs_sem, xr_sem, ys_sem, yr_sem, zs_sem, zr_sem, fs_sem, fr_sem, gs_sem, gr_sem,
 ):
     nx, ny, nz = sizes
     size = dict(zip(AXES, sizes))
+    direct = reaches(sizes)
     me = {name: lax.axis_index(name) for name in AXES}
 
     def there(name, step):
@@ -159,11 +166,13 @@
         return copy
 
     barrier = pltpu.get_barrier_semaphore()
-    for name in AXES:
-        for step in range(1, size[name]):
-            pl.semaphore_signal(
-                barrier, inc=1, device_id=there(name, step), device_id_type=pl.DeviceIdType.MESH
-            )
+    greeted = [(name, step) for name in AXES for step in (1, -1)]
+    if not direct:
+        greeted = [(name, step) for name in AXES for step in range(1, size[name])]
+    for name, step in greeted:
+        pl.semaphore_signal(
+            barrier, inc=1, device_id=there(name, step), device_id_type=pl.DeviceIdType.MESH
+        )
     local = {}
     for a, ref in enumerate((it_ref, src_ref, perm_ref, store_ref)):
         local[a] = pltpu.make_async_copy(ref, I.at[a], lsem.at[a])
@@ -182,7 +191,7 @@
             D[b, t, LAST:ROWS, :] = jnp.zeros((ROWS - LAST, 128), F32)
     for a in range(4):
         local[a].wait()
-    pl.semaphore_wait(barrier, nx + ny + nz - 3)
+    pl.semaphore_wait(barrier, len(greeted))
 
     sent = []
     xcopy, ycopy, zcopy = {}, {}, {}
@@ -308,21 +317,56 @@
             copy.wait_recv()
         sent.extend(copies)
 
-    GS[...] = tile
-    gather(GS, GZ, "gz", 0)
-    wlane = iota((8, width), 1)
-    merged = None
-    for z in range(nz):
-        part = GZ[z]
-        if width > 128:
-            part = jnp.concatenate([part] * (width // 128), axis=1)
-        merged = part if merged is None else jnp.where((wlane // 16) % nz == z, part, merged)
-    GM[...] = merged
-    gather(GM, GY, "gy", nz - 1)
-    for y in range(ny):
-        for q in range(4):
-            GV[8 * q + 2 * y : 8 * q + 2 * y + 2, :] = GY[y, 2 * q : 2 * q + 2, :]
-    gather(GV, GX, "gx", nz + ny - 2)
+    if direct:
+        def at(i, j, k):
+            return (i * ny + j) * nz + k
+
+        GS[...] = tile
+        mine = at(*[me[name] for name in AXES])
+        copies = []
+        for i in range(nx):
+            for j in range(ny):
+                for k in range(nz):
+                    if i + j + k:
+                        copy = pltpu.make_async_remote_copy(
+                            src_ref=GS, dst_ref=GA.at[mine],
+                            send_sem=gs_sem.at[len(copies)], recv_sem=gr_sem.at[len(copies)],
+                            device_id=tuple(
+                                lax.rem(me[name] + step, size[name])
+                                for name, step in zip(AXES, (i, j, k))
+                            ),
+                            device_id_type=pl.DeviceIdType.MESH,
+                        )
+                        copy.start()
+                        copies.append(copy)
+        GA[mine] = tile
+        for copy in copies:
+            copy.wait_recv()
+        sent.extend(copies)
+        wlane = iota((8, 128), 1)
+        for i in range(nx):
+            for j in range(ny):
+                merged = GA[at(i, j, 0)]
+                for k in range(1, nz):
+                    merged = jnp.where((wlane // 16) % nz == k, GA[at(i, j, k)], merged)
+                for q in range(4):
+                    GX[i, 8 * q + 2 * j : 8 * q + 2 * j + 2, :] = merged[2 * q : 2 * q + 2, :]
+    else:
+        GS[...] = tile
+        gather(GS, GZ, "gz", 0)
+        wlane = iota((8, width), 1)
+        merged = None
+        for z in range(nz):
+            part = GZ[z]
+            if width > 128:
+                part = jnp.concatenate([part] * (width // 128), axis=1)
+            merged = part if merged is None else jnp.where((wlane // 16) % nz == z, part, merged)
+        GM[...] = merged
+        gather(GM, GY, "gy", nz - 1)
+        for y in range(ny):
+            for q in range(4):
+                GV[8 * q + 2 * y : 8 * q + 2 * y + 2, :] = GY[y, 2 * q : 2 * q + 2, :]
+        gather(GV, GX, "gx", nz + ny - 2)
 
     base = [GX[i, 0:8, :] for i in range(nx)]
     cres = [GX[i, 8:16, :] for i in range(nx)]
@@ -355,7 +399,8 @@
     nx, ny, nz = sizes
     width = max(128, 16 * nz)
     field = lambda *lead: pltpu.VMEM(lead + (3, ROWS, 128), F32)
-    links = nx + ny + nz - 3
+    direct = reaches(sizes)
+    links = nx * ny * nz - 1 if direct else nx + ny + nz - 3
     scratch = [
         pltpu.VMEM((4, 128, 128), F32),
         pltpu.VMEM((4, 2, 64, 128), F32),
@@ -372,6 +417,7 @@
         pltpu.VMEM((16, 128), F32),
         pltpu.VMEM((2, 16, 128), F32),
         pltpu.VMEM((8, 128), F32),
+        pltpu.VMEM((nx * ny * nz if direct else 1, 8, 128), F32),
         pltpu.VMEM((nz, 8, 128), F32),
         pltpu.VMEM((8, width), F32),
         pltpu.VMEM((ny, 8, width), F32),
@@ -386,7 +432,7 @@
         out_specs=pl.BlockSpec(memory_space=pltpu.VMEM),
         scratch_shapes=scratch,
         compiler_params=pltpu.CompilerParams(
-            collective_id=0, has_side_effects=True, vmem_limit_bytes=24 * 1024 * 1024
+            collective_id=0, has_side_effects=True, vmem_limit_bytes=60 * 1024 * 1024
         ),
     )(*[x.reshape(128, 128) for x in args])
     return out.reshape(8, 16, 128)

time: 40.7 us -> 35.3 us (0.87)
  Pallas kernels: 36.4 us -> 33.6 us
  local copies, waits for them, and re-layouts: 3.99 us -> 1.47 us
    pallas_call x1, Pallas kernels: 36.4 us -> 33.6 us  [shards(): pl.pallas_call(functools.partial(kernel, sizes), out_shape=jax.ShapeDtype...]
    unnamed x9 -> x1, local copies, waits for them, and re-layouts: 3.99 us -> 1.47 us
where the time goes in v2:
time: 35.3 us; the launch traced here: 35.1 us
  Pallas kernels  33.6 us (95%)
  local copies, waits for them, and re-layouts  1.47 us (4%)
    pallas_call x1, Pallas kernels, shards(): pl.pallas_call(functools.partial(kernel, sizes), out_shape=jax.ShapeDtype...  33.6 us
    unnamed x1, local copies, waits for them, and re-layouts  1.47 us

profile of v2, /device:TPU:0, one launch (start us, length us, event | category | flops | bytes accessed | tf_op | source)
XLA Modules:
  0.0 35.1 jit_solution(1501296143942272845)
XLA Ops:
  0.0 33.6 %shard_map.46 = f32[128,128]{1,0:T(8,128)} custom-call(f32[128,128]{1,0:T(8,128)} %bitcast.6, f32[128,128]{1,0:T(8,128)} %bitcast.7, f32[128,128]{1,0:T(8,128)} %bitcast.8, f32[128,128]{1,0:T(8,128)} %bitcast.9), custom_call_target="tpu_custom_call" | custom-call | tf_op jit(solution)/shard_map/pallas_call | solution.py:428
  33.6 1.5 %copy.6 = f32[8,16,128]{2,1,0:T(8,128)} copy(f32[8,16,128]{2,1,0:T(8,128)} %bitcast.5) | data formatting | bytes 131072

commit v3 on v2

--- a/solution.py
+++ b/solution.py
@@ -145,9 +145,9 @@
 
 def kernel(
     sizes, it_ref, src_ref, perm_ref, store_ref, out,
-    I, XR, PA, T, ZS, ZR, AX, AY, AZ, FZ, RES, RD, D, Q, CB, XS, XF, YF, FS, ZF,
+    I, XR, XP, PR, PA, T, ZS, ZR, AX, AY, AZ, FZ, RES, RD, D, Q, CB, XS, XF, YF, FS, ZF,
     GS, GA, GZ, GM, GY, GV, GX, CR,
-    lsem, xs_sem, xr_sem, ys_sem, yr_sem, zs_sem, zr_sem, fs_sem, fr_sem, gs_sem, gr_sem,
+    lsem, xs_sem, xr_sem, ys_sem, yr_sem, ps_sem, pr_sem, zs_sem, zr_sem, fs_sem, fr_sem, gs_sem, gr_sem,
 ):
     nx, ny, nz = sizes
     size = dict(zip(AXES, sizes))
@@ -195,28 +195,82 @@
 
     sent = []
     xcopy, ycopy, zcopy = {}, {}, {}
-    for a in ORDER:
-        hi = send(I.at[a, pl.ds(64, 64)], XR.at[a, 0], xs_sem.at[2 * a], xr_sem.at[2 * a], "gx", 1)
-        lo = send(I.at[a, pl.ds(0, 64)], XR.at[a, 1], xs_sem.at[2 * a + 1], xr_sem.at[2 * a + 1], "gx", -1)
-        xcopy[a] = (hi, lo)
-        sent += [hi, lo]
-    for a in ORDER:
+
+    def fill_own(a):
         for x in range(8):
             PA[a, pl.ds(64 + 4 + x, 16, stride=16), :] = I[a, 16 * x : 16 * x + 16, :]
-    for a in ORDER:
+
+    def send_x(a, planes):
+        n = 16 * planes
+        hi = send(I.at[a, pl.ds(128 - n, n)], XR.at[a, 0, pl.ds(64 - n, n)], xs_sem.at[2 * a], xr_sem.at[2 * a], "gx", 1)
+        lo = send(I.at[a, pl.ds(0, n)], XR.at[a, 1, pl.ds(0, n)], xs_sem.at[2 * a + 1], xr_sem.at[2 * a + 1], "gx", -1)
+        xcopy[a] = (hi, lo)
+        sent.extend([hi, lo])
+
+    def fill_x(a, planes):
         for side in range(2):
             xcopy[a][side].wait_recv()
-            for x in range(4):
+            for x in range(4 - planes, 4) if side == 0 else range(planes):
                 PA[a, pl.ds(64 + 12 * side + x, 16, stride=16), :] = XR[a, side, 16 * x : 16 * x + 16, :]
+
+    def send_y(a):
         hi = send(PA.at[a, pl.ds(256, 64)], PA.at[a, pl.ds(0, 64)], ys_sem.at[2 * a], yr_sem.at[2 * a], "gy", 1)
         lo = send(PA.at[a, pl.ds(64, 64)], PA.at[a, pl.ds(320, 64)], ys_sem.at[2 * a + 1], yr_sem.at[2 * a + 1], "gy", -1)
         ycopy[a] = (hi, lo)
-        sent += [hi, lo]
+
+    first, second = ORDER[:2], ORDER[2:]
+    for a in first:
+        send_x(a, 4)
+    for a in second:
+        fill_own(a)
+        for x in (0, 15):
+            PA[a, pl.ds(64 + x, 16, stride=16), :] = jnp.zeros((16, 128), F32)
+        send_y(a)
+    for a in second:
+        send_x(a, 3)
+    for a in first:
+        fill_own(a)
+    pieces = {}
+    for n, a in enumerate(second):
+        for copy in ycopy[a]:
+            copy.wait_recv()
+        for p in range(3):
+            for side in range(2):
+                x = (9, 4)[side] + p
+                XP[n, side, 8 * p : 8 * p + 4, :] = PA[a, pl.ds(x, 4, stride=16), :]
+                XP[n, side, 8 * p + 4 : 8 * p + 8, :] = PA[a, pl.ds(320 + x, 4, stride=16), :]
+        pieces[a] = [
+            send(XP.at[n, side], PR.at[n, side], ps_sem.at[2 * n + side], pr_sem.at[2 * n + side], "gx", (1, -1)[side])
+            for side in range(2)
+        ]
+        sent.extend(pieces[a])
+    for a in first:
+        fill_x(a, 4)
+        send_y(a)
+        sent.extend(ycopy[a])
+
+    def arrive(n, a):
+        if a in first:
+            for copy in ycopy[a]:
+                copy.wait_recv()
+            return
+        for copy in ycopy[a]:
+            copy.wait_send()
+        fill_x(a, 3)
+        for side in range(2):
+            pieces[a][side].wait_recv()
+            for p in range(3):
+                x = (1, 12)[side] + p
+                PA[a, pl.ds(x, 4, stride=16), :] = PR[n, side, 8 * p : 8 * p + 4, :]
+                PA[a, pl.ds(320 + x, 4, stride=16), :] = PR[n, side, 8 * p + 4 : 8 * p + 8, :]
+        for x in (0, 15):
+            PA[a, pl.ds(x, 4, stride=16), :] = jnp.zeros((4, 128), F32)
+            PA[a, pl.ds(320 + x, 4, stride=16), :] = jnp.zeros((4, 128), F32)
+
     for p in range(2):
         for h in range(2):
             a = ORDER[2 * p + h]
-            ycopy[a][0].wait_recv()
-            ycopy[a][1].wait_recv()
+            arrive(h, a)
             for t in range(3):
                 m = PA[a, 128 * t : 128 * t + 128, :].T
                 T[a, t, 12:140, :] = m
@@ -404,6 +458,8 @@
     scratch = [
         pltpu.VMEM((4, 128, 128), F32),
         pltpu.VMEM((4, 2, 64, 128), F32),
+        pltpu.VMEM((2, 2, 24, 128), F32),
+        pltpu.VMEM((2, 2, 24, 128), F32),
         pltpu.VMEM((4, 384, 128), F32),
         field(4),
         pltpu.VMEM((2, 2, 3, 8, 128), F32),
@@ -424,7 +480,7 @@
         pltpu.VMEM((32, width), F32),
         pltpu.VMEM((nx, 32, width), F32),
         pltpu.VMEM((nx, 8, width), F32),
-    ] + [pltpu.SemaphoreType.DMA((n,)) for n in (4, 8, 8, 8, 8, 4, 4, 6, 6, links, links)]
+    ] + [pltpu.SemaphoreType.DMA((n,)) for n in (4, 8, 8, 8, 8, 4, 4, 4, 4, 6, 6, links, links)]
     out = pl.pallas_call(
         functools.partial(kernel, sizes),
         out_shape=jax.ShapeDtypeStruct((128, 128), F32),

time: 35.3 us -> 34 us (0.963)
  Pallas kernels: 33.6 us -> 32.3 us
    pallas_call x1, Pallas kernels: 33.6 us -> 32.3 us  [shards(): pl.pallas_call(functools.partial(kernel, sizes), out_shape=jax.ShapeDtype...]
where the time goes in v3:
time: 34 us; the launch traced here: 33.8 us
  Pallas kernels  32.3 us (95%)
  local copies, waits for them, and re-layouts  1.47 us (4%)
    pallas_call x1, Pallas kernels, shards(): pl.pallas_call(functools.partial(kernel, sizes), out_shape=jax.ShapeDtype...  32.3 us
    unnamed x1, local copies, waits for them, and re-layouts  1.47 us

profile of v3, /device:TPU:0, one launch (start us, length us, event | category | flops | bytes accessed | tf_op | source)
XLA Modules:
  0.0 33.8 jit_solution(6983010482561258197)
XLA Ops:
  0.0 32.3 %shard_map.46 = f32[128,128]{1,0:T(8,128)} custom-call(f32[128,128]{1,0:T(8,128)} %bitcast.6, f32[128,128]{1,0:T(8,128)} %bitcast.7, f32[128,128]{1,0:T(8,128)} %bitcast.8, f32[128,128]{1,0:T(8,128)} %bitcast.9), custom_call_target="tpu_custom_call" | custom-call | tf_op jit(solution)/shard_map/pallas_call | solution.py:484
  32.3 1.5 %copy.6 = f32[8,16,128]{2,1,0:T(8,128)} copy(f32[8,16,128]{2,1,0:T(8,128)} %bitcast.5) | data formatting | bytes 131072

commit v4 on v3

--- a/solution.py
+++ b/solution.py
@@ -15,7 +15,7 @@
 ROWS = 152
 FIRST = 8
 LAST = 144
-CHUNK = 16
+CHUNK = 48
 ITER, SRC, PERM, STORE = 0, 1, 2, 3
 ORDER = (ITER, PERM, SRC, STORE)
 
@@ -140,13 +140,13 @@
 def reaches(sizes):
     rx, ry, rz = (n // 2 for n in sizes)
     spare = max(rx - 1, 0) + max(ry - 1, 0) + max(rz - 1, 0)
-    return spare <= 2 and 16 * sizes[2] <= 128
+    return spare <= 2 and 128 % (16 * sizes[2]) == 0
 
 
 def kernel(
     sizes, it_ref, src_ref, perm_ref, store_ref, out,
     I, XR, XP, PR, PA, T, ZS, ZR, AX, AY, AZ, FZ, RES, RD, D, Q, CB, XS, XF, YF, FS, ZF,
-    GS, GA, GZ, GM, GY, GV, GX, CR,
+    GS, GL, GA, GZ, GM, GY, GV, GX, CR,
     lsem, xs_sem, xr_sem, ys_sem, yr_sem, ps_sem, pr_sem, zs_sem, zr_sem, fs_sem, fr_sem, gs_sem, gr_sem,
 ):
     nx, ny, nz = sizes
@@ -375,7 +375,8 @@
         def at(i, j, k):
             return (i * ny + j) * nz + k
 
-        GS[...] = tile
+        own = iota((8, 128), 0) == iota((8, 128), 1) // 16
+        GL[...] = jnp.sum(jnp.where(own, tile, 0.0), axis=0, keepdims=True)
         mine = at(*[me[name] for name in AXES])
         copies = []
         for i in range(nx):
@@ -383,7 +384,7 @@
                 for k in range(nz):
                     if i + j + k:
                         copy = pltpu.make_async_remote_copy(
-                            src_ref=GS, dst_ref=GA.at[mine],
+                            src_ref=GL, dst_ref=GA.at[mine],
                             send_sem=gs_sem.at[len(copies)], recv_sem=gr_sem.at[len(copies)],
                             device_id=tuple(
                                 lax.rem(me[name] + step, size[name])
@@ -393,16 +394,27 @@
                         )
                         copy.start()
                         copies.append(copy)
-        GA[mine] = tile
+        GA[mine] = GL[...]
         for copy in copies:
             copy.wait_recv()
         sent.extend(copies)
-        wlane = iota((8, 128), 1)
+        block = iota((8, 128), 0) == iota((8, 128), 1) // 16
+        m, l = iota((128, 128), 0), iota((128, 128), 1)
+        placed = 0.0
+        for k in range(nz):
+            lines = [
+                jnp.where(block, jnp.broadcast_to(GA[at(i, j, k)], (8, 128)), 0.0)
+                for i in range(nx) for j in range(ny)
+            ]
+            move = jnp.where((l // 16) % nz == k, jnp.where(l % 16 == m % 16, 1.0, 0.0), 0.0)
+            placed = placed + jnp.dot(
+                jnp.concatenate(lines, axis=0), move.astype(F32),
+                precision=lax.Precision.HIGHEST, preferred_element_type=F32,
+            )
         for i in range(nx):
             for j in range(ny):
-                merged = GA[at(i, j, 0)]
-                for k in range(1, nz):
-                    merged = jnp.where((wlane // 16) % nz == k, GA[at(i, j, k)], merged)
+                at_row = 8 * (i * ny + j)
+                merged = placed[at_row : at_row + 8, :]
                 for q in range(4):
                     GX[i, 8 * q + 2 * j : 8 * q + 2 * j + 2, :] = merged[2 * q : 2 * q + 2, :]
     else:
@@ -473,7 +485,8 @@
         pltpu.VMEM((16, 128), F32),
         pltpu.VMEM((2, 16, 128), F32),
         pltpu.VMEM((8, 128), F32),
-        pltpu.VMEM((nx * ny * nz if direct else 1, 8, 128), F32),
+        pltpu.VMEM((1, 128), F32),
+        pltpu.VMEM((nx * ny * nz if direct else 1, 1, 128), F32),
         pltpu.VMEM((nz, 8, 128), F32),
         pltpu.VMEM((8, width), F32),
         pltpu.VMEM((ny, 8, width), F32),

time: 34 us -> 32.8 us (0.965)
  Pallas kernels: 32.3 us -> 31.1 us
    pallas_call x1, Pallas kernels: 32.3 us -> 31.1 us  [shards(): pl.pallas_call(functools.partial(kernel, sizes), out_shape=jax.ShapeDtype...]
where the time goes in v4:
time: 32.8 us; the launch traced here: 32.6 us
  Pallas kernels  31.1 us (95%)
  local copies, waits for them, and re-layouts  1.47 us (4%)
    pallas_call x1, Pallas kernels, shards(): pl.pallas_call(functools.partial(kernel, sizes), out_shape=jax.ShapeDtype...  31.1 us
    unnamed x1, local copies, waits for them, and re-layouts  1.47 us

profile of v4, /device:TPU:0, one launch (start us, length us, event | category | flops | bytes accessed | tf_op | source)
XLA Modules:
  0.0 32.6 jit_solution(8619821671844579323)
XLA Ops:
  0.0 31.1 %shard_map.46 = f32[128,128]{1,0:T(8,128)} custom-call(f32[128,128]{1,0:T(8,128)} %bitcast.6, f32[128,128]{1,0:T(8,128)} %bitcast.7, f32[128,128]{1,0:T(8,128)} %bitcast.8, f32[128,128]{1,0:T(8,128)} %bitcast.9), custom_call_target="tpu_custom_call" | custom-call | tf_op jit(solution)/shard_map/pallas_call | solution.py:497
  31.1 1.5 %copy.6 = f32[8,16,128]{2,1,0:T(8,128)} copy(f32[8,16,128]{2,1,0:T(8,128)} %bitcast.5) | data formatting | bytes 131072
